TPU v7x, 128 devices: a whole 4x4x4 slice. The times are simulated.
128 devices in a mesh: fsdp: 4 (over y_lo, core), sp: 8 (over y_hi, x), tp: 4 (over z).
Axes of the slice: x: 4, y: 4 (y_hi: 2, y_lo: 2; y = y_hi * 2 + y_lo), z: 4, core: 2. Of those that a mesh axis runs over, the one named last changes fastest.
Arguments:
- tokens: bfloat16 [8, 2048, 2048], P('fsdp', 'sp'), may hold values from -6 to 6
- ln_gain: bfloat16 [2048], replicated, may hold values from 0.5 to 1.5
- ln_bias: bfloat16 [2048], replicated, may hold values from -1.25 to 1.25
- w_qkv: bfloat16 [2048, 3, 2048], P(('fsdp', 'sp'), None, 'tp'), may hold values from -0.1875 to 0.1875
- b_qkv: bfloat16 [3, 2048], P(None, 'tp'), may hold values from -1.75 to 1.75
- w_dense: bfloat16 [2048, 2048], P('tp', ('fsdp', 'sp')), may hold values from -1 to 1
- b_dense: bfloat16 [2048], replicated, may hold values from -3 to 3
- w_fc1: bfloat16 [2048, 8192], P(('fsdp', 'sp'), 'tp'), may hold values from -0.125 to 0.125
- b_fc1: bfloat16 [8192], P('tp'), may hold values from -1.75 to 1.75
- w_fc2: bfloat16 [8192, 2048], P('tp', ('fsdp', 'sp')), may hold values from -0.09375 to 0.09375
- b_fc2: bfloat16 [2048], replicated, may hold values from -3 to 3
- cotangent: bfloat16 [8, 2048, 2048], P('fsdp', 'sp'), may hold values from -6 to 6
Outputs:
- mixed_out: bfloat16 [8, 2048, 2048], P('fsdp', 'sp')
- grad_tokens: bfloat16 [8, 2048, 2048], P('fsdp', 'sp')
- grad_ln_gain: float32 [2048], replicated
- grad_ln_bias: float32 [2048], replicated
- grad_w_qkv: float32 [2048, 3, 2048], P(('fsdp', 'sp'), None, 'tp')
- grad_b_qkv: float32 [3, 2048], P(None, 'tp')
- grad_w_dense: float32 [2048, 2048], P('tp', ('fsdp', 'sp'))
- grad_b_dense: float32 [2048], replicated
- grad_w_fc1: float32 [2048, 8192], P(('fsdp', 'sp'), 'tp')
- grad_b_fc1: float32 [8192], P('tp')
- grad_w_fc2: float32 [8192, 2048], P('tp', ('fsdp', 'sp'))
- grad_b_fc2: float32 [2048], replicated
All inputs are finite; a program needn't handle non-finite values.
Results may differ from a plain program's by a relative error of at most 0.023.
Values may be sent and summed in bfloat16 or wider, within the bound.
A program may use at most 192 MiB of HBM per device.

v0:
```python
import math

import jax
import jax.numpy as jnp
from jax import lax
from jax.sharding import PartitionSpec as P

HDIM = 64
ROT = 32


big_negative = -1e30


def layer_norm(inputs, gain, shift):
    average = jnp.mean(inputs, axis=-1, keepdims=True)
    centered = inputs - average
    spread = jnp.mean(centered * centered, axis=-1, keepdims=True)
    return centered * lax.rsqrt(spread + 1e-05) * gain + shift


def rotate(part, cosine, sine):
    half = ROT // 2
    first_half = part[..., :half]
    second_half = part[..., half:ROT]
    remain = part[..., ROT:]
    return jnp.concatenate(
        [
            first_half * cosine - second_half * sine,
            second_half * cosine + first_half * sine,
            remain,
        ],
        axis=-1,
    )


def contract_last(left, right):
    return lax.dot_general(
        left, right, (((1,), (1,)), ((), ())), preferred_element_type=jnp.float32
    )


def contract_first(left, right):
    return lax.dot_general(
        left, right, (((0,), (0,)), ((), ())), preferred_element_type=jnp.float32
    )


def masked_scores(q_block, k_prefix, begin_at, factor):
    scores = (
        jnp.einsum("sqhd,skhd->shqk", q_block, k_prefix, preferred_element_type=jnp.float32)
        * factor
    )
    q_places = begin_at + jnp.arange(q_block.shape[1], dtype=jnp.int32)
    k_places = jnp.arange(k_prefix.shape[1], dtype=jnp.int32)
    causal = q_places[:, None] >= k_places[None, :]
    return jnp.where(causal[None, None], scores, big_negative)


def attend_forward(q_all, k_all, v_all, factor):
    length = q_all.shape[1]
    block = min(512, length)
    results = []
    log_totals = []
    for begin_at in range(0, length, block):
        stop_at = begin_at + block
        scores = masked_scores(q_all[:, begin_at:stop_at], k_all[:, :stop_at], begin_at, factor)
        row_top = jnp.max(scores, axis=-1, keepdims=True)
        weights = jnp.exp(scores - row_top)
        row_total = jnp.sum(weights, axis=-1, keepdims=True)
        probs = (weights / row_total).astype(jnp.bfloat16)
        results.append(
            jnp.einsum(
                "shqk,skhd->sqhd", probs, v_all[:, :stop_at], preferred_element_type=jnp.float32
            )
        )
        log_totals.append(row_top + jnp.log(row_total))
    return (
        jnp.concatenate(results, axis=1).astype(jnp.bfloat16),
        jnp.concatenate(log_totals, axis=2),
    )


def attend_backward(q_all, k_all, v_all, log_totals, grad_heads, factor):
    length = q_all.shape[1]
    block = min(512, length)
    grad_query = []
    grad_key = jnp.zeros(k_all.shape, jnp.float32)
    grad_value = jnp.zeros(v_all.shape, jnp.float32)
    for begin_at in range(0, length, block):
        stop_at = begin_at + block
        q_block = q_all[:, begin_at:stop_at]
        g_block = grad_heads[:, begin_at:stop_at]
        scores = masked_scores(q_block, k_all[:, :stop_at], begin_at, factor)
        probs = jnp.exp(scores - log_totals[:, :, begin_at:stop_at])
        grad_probs = jnp.einsum(
            "sqhd,skhd->shqk", g_block, v_all[:, :stop_at], preferred_element_type=jnp.float32
        )
        inner_dot = jnp.sum(probs * grad_probs, axis=-1, keepdims=True)
        grad_scores = (probs * (grad_probs - inner_dot)).astype(jnp.bfloat16)
        grad_query.append(
            (
                jnp.einsum(
                    "shqk,skhd->sqhd",
                    grad_scores,
                    k_all[:, :stop_at],
                    preferred_element_type=jnp.float32,
                )
                * factor
            ).astype(jnp.bfloat16)
        )
        grad_key = grad_key.at[:, :stop_at].add(
            jnp.einsum("shqk,sqhd->skhd", grad_scores, q_block, preferred_element_type=jnp.float32)
            * factor
        )
        grad_value = grad_value.at[:, :stop_at].add(
            jnp.einsum(
                "shqk,sqhd->skhd",
                probs.astype(jnp.bfloat16),
                g_block,
                preferred_element_type=jnp.float32,
            )
        )
    return (
        jnp.concatenate(grad_query, axis=1),
        grad_key.astype(jnp.bfloat16),
        grad_value.astype(jnp.bfloat16),
    )


def body(
    tokens, ln_gain, ln_bias, w_qkv, b_qkv, w_dense, b_dense, w_fc1, b_fc1, w_fc2, b_fc2, cotangent
):
    seq_count, local_len, model_width = tokens.shape
    row_count = seq_count * local_len
    heads_tp = w_qkv.shape[2] // HDIM
    factor = HDIM ** (-0.5)
    fwd_qkv, fwd_dense, fwd_fc1, fwd_fc2 = (
        lax.all_gather(w_qkv, ("fsdp", "sp"), axis=0, tiled=True),
        lax.all_gather(w_dense, ("fsdp", "sp"), axis=1, tiled=True),
        lax.all_gather(w_fc1, ("fsdp", "sp"), axis=0, tiled=True),
        lax.all_gather(w_fc2, ("fsdp", "sp"), axis=1, tiled=True),
    )
    flat_qkv = fwd_qkv.reshape(model_width, 3 * heads_tp * HDIM)
    gain = ln_gain.astype(jnp.float32)
    shift = ln_bias.astype(jnp.float32)
    x_rows = tokens.reshape(row_count, model_width).astype(jnp.float32)
    normed = layer_norm(x_rows, gain, shift)
    hidden = normed.astype(jnp.bfloat16)
    projected = jnp.dot(hidden, flat_qkv, preferred_element_type=jnp.float32) + b_qkv.astype(
        jnp.float32
    ).reshape(-1)
    projected = projected.reshape(seq_count, local_len, 3, heads_tp, HDIM)
    offset = lax.axis_index("sp") * local_len
    places = (offset + jnp.arange(local_len, dtype=jnp.int32)).astype(jnp.float32)
    freqs = jnp.exp(jnp.arange(ROT // 2, dtype=jnp.float32) * (-2.0 * math.log(10000.0) / ROT))
    angle = places[:, None, None] * freqs[None, None, :]
    cosine = jnp.cos(angle)
    sine = jnp.sin(angle)
    query = rotate(projected[:, :, 0], cosine, sine).astype(jnp.bfloat16)
    key_part = rotate(projected[:, :, 1], cosine, sine).astype(jnp.bfloat16)
    value = projected[:, :, 2].astype(jnp.bfloat16)
    q_all, k_all, v_all = (
        lax.all_to_all(query, "sp", split_axis=2, concat_axis=1, tiled=True),
        lax.all_to_all(key_part, "sp", split_axis=2, concat_axis=1, tiled=True),
        lax.all_to_all(value, "sp", split_axis=2, concat_axis=1, tiled=True),
    )
    inner = jnp.dot(hidden, fwd_fc1, preferred_element_type=jnp.float32) + b_fc1.astype(jnp.float32)
    active_low = jax.nn.gelu(inner, approximate=True).astype(jnp.bfloat16)
    mlp_part = jnp.dot(active_low, fwd_fc2, preferred_element_type=jnp.float32)
    mlp_summed = lax.psum(mlp_part.astype(jnp.bfloat16), "tp").astype(jnp.float32)
    heads_out, log_totals = attend_forward(q_all, k_all, v_all, factor)
    out_local = lax.all_to_all(heads_out, "sp", split_axis=1, concat_axis=2, tiled=True)
    attended = out_local.reshape(row_count, heads_tp * HDIM)
    attn_part = jnp.dot(attended, fwd_dense, preferred_element_type=jnp.float32)
    branch_total = lax.psum(attn_part.astype(jnp.bfloat16), "tp").astype(jnp.float32) + mlp_summed
    mixed_out = (
        (x_rows + branch_total + b_dense.astype(jnp.float32) + b_fc2.astype(jnp.float32))
        .astype(jnp.bfloat16)
        .reshape(tokens.shape)
    )
    back_qkv, back_dense, back_fc1, back_fc2 = (
        lax.all_gather(w_qkv, ("fsdp", "sp"), axis=0, tiled=True),
        lax.all_gather(w_dense, ("fsdp", "sp"), axis=1, tiled=True),
        lax.all_gather(w_fc1, ("fsdp", "sp"), axis=0, tiled=True),
        lax.all_gather(w_fc2, ("fsdp", "sp"), axis=1, tiled=True),
    )
    back_flat = back_qkv.reshape(model_width, 3 * heads_tp * HDIM)
    grad_rows = cotangent.reshape(row_count, model_width)
    grad_attended = (
        contract_last(grad_rows, back_dense)
        .astype(jnp.bfloat16)
        .reshape(seq_count, local_len, heads_tp, HDIM)
    )
    grad_heads = lax.all_to_all(grad_attended, "sp", split_axis=2, concat_axis=1, tiled=True)
    grad_active = contract_last(grad_rows, back_fc2)
    gelu_pull = jax.vjp(lambda values: jax.nn.gelu(values, approximate=True), inner)[1]
    grad_inner = gelu_pull(grad_active)[0].astype(jnp.bfloat16)
    grad_w_fc2 = contract_first(active_low, grad_rows)
    grad_w_dense = contract_first(attended, grad_rows)
    grad_w_fc1 = contract_first(hidden, grad_inner)
    grad_query, grad_key, grad_value = attend_backward(
        q_all, k_all, v_all, log_totals, grad_heads, factor
    )
    back_query, back_key, back_value = (
        lax.all_to_all(grad_query, "sp", split_axis=1, concat_axis=2, tiled=True),
        lax.all_to_all(grad_key, "sp", split_axis=1, concat_axis=2, tiled=True),
        lax.all_to_all(grad_value, "sp", split_axis=1, concat_axis=2, tiled=True),
    )
    grad_projected = jnp.stack(
        [
            rotate(back_query.astype(jnp.float32), cosine, -sine),
            rotate(back_key.astype(jnp.float32), cosine, -sine),
            back_value.astype(jnp.float32),
        ],
        axis=2,
    )
    grad_projected = grad_projected.astype(jnp.bfloat16).reshape(row_count, 3 * heads_tp * HDIM)
    grad_w_qkv = contract_first(hidden, grad_projected).reshape(model_width, 3, heads_tp * HDIM)
    norm_part = contract_last(grad_projected, back_flat) + contract_last(grad_inner, back_fc1)
    grad_normed = lax.psum(norm_part.astype(jnp.bfloat16), "tp").astype(jnp.float32)
    norm_pull = jax.vjp(layer_norm, x_rows, gain, shift)[1]
    grad_x, grad_gain_local, grad_shift_local = norm_pull(grad_normed)
    grad_tokens = (
        (grad_rows.astype(jnp.float32) + grad_x).astype(jnp.bfloat16).reshape(tokens.shape)
    )
    bias_qkv_local = jnp.sum(grad_projected.astype(jnp.float32), axis=0).reshape(3, heads_tp * HDIM)
    bias_fc1_local = jnp.sum(grad_inner.astype(jnp.float32), axis=0)
    bias_out_local = jnp.sum(grad_rows.astype(jnp.float32), axis=0)
    grad_gain, grad_shift, grad_b_qkv, grad_b_fc1, grad_b_out = (
        lax.psum(grad_gain_local.astype(jnp.bfloat16), ("fsdp", "sp")).astype(jnp.float32),
        lax.psum(grad_shift_local.astype(jnp.bfloat16), ("fsdp", "sp")).astype(jnp.float32),
        lax.psum(bias_qkv_local.astype(jnp.bfloat16), ("fsdp", "sp")).astype(jnp.float32),
        lax.psum(bias_fc1_local.astype(jnp.bfloat16), ("fsdp", "sp")).astype(jnp.float32),
        lax.psum(bias_out_local.astype(jnp.bfloat16), ("fsdp", "sp")).astype(jnp.float32),
    )
    shard_qkv, shard_dense, shard_fc1, shard_fc2 = (
        lax.psum_scatter(
            grad_w_qkv.astype(jnp.bfloat16), ("fsdp", "sp"), scatter_dimension=0, tiled=True
        ).astype(jnp.float32),
        lax.psum_scatter(
            grad_w_dense.astype(jnp.bfloat16), ("fsdp", "sp"), scatter_dimension=1, tiled=True
        ).astype(jnp.float32),
        lax.psum_scatter(
            grad_w_fc1.astype(jnp.bfloat16), ("fsdp", "sp"), scatter_dimension=0, tiled=True
        ).astype(jnp.float32),
        lax.psum_scatter(
            grad_w_fc2.astype(jnp.bfloat16), ("fsdp", "sp"), scatter_dimension=1, tiled=True
        ).astype(jnp.float32),
    )
    return (
        mixed_out,
        grad_tokens,
        grad_gain,
        grad_shift,
        shard_qkv,
        grad_b_qkv,
        shard_dense,
        grad_b_out,
        shard_fc1,
        grad_b_fc1,
        shard_fc2,
        grad_b_out,
    )


def solution(mesh):
    in_specs = (
        P("fsdp", "sp", None),
        P(),
        P(),
        P(("fsdp", "sp"), None, "tp"),
        P(None, "tp"),
        P("tp", ("fsdp", "sp")),
        P(),
        P(("fsdp", "sp"), "tp"),
        P("tp"),
        P("tp", ("fsdp", "sp")),
        P(),
        P("fsdp", "sp", None),
    )
    out_specs = (
        P("fsdp", "sp", None),
        P("fsdp", "sp", None),
        P(),
        P(),
        P(("fsdp", "sp"), None, "tp"),
        P(None, "tp"),
        P("tp", ("fsdp", "sp")),
        P(),
        P(("fsdp", "sp"), "tp"),
        P("tp"),
        P("tp", ("fsdp", "sp")),
        P(),
    )
    return jax.shard_map(body, mesh=mesh, in_specs=in_specs, out_specs=out_specs, check_vma=False)
```

profile of v0, /device:TPU:24, one launch (start us, length us, event | category | flops | bytes accessed | tf_op | source)
XLA Modules:
  0.0 1251.5 jit_solution(7794790815522057469)
XLA Ops:
  19.6 73.8 %all-gather.7.cloned.1.call-done = bf16[512,2048]{0,1:T(8,128)(2,1)} async-done(((bf16[512,64]{0,1:T(8,128)(2,1)}), bf16[512,2048]{0,1:T(8,128)(2,1)}) %all-gather.7.cloned.1.call-update) | async-done | bytes 2097168 | tf_op jit(solution)/shard_map/all_gather | solution.py:140
  93.4 3.5 convolution_convert_fusion.6
  98.0 7.5 all-to-all-start.4
  105.5 85.1 %all-gather.5.cloned.1.call-done = bf16[2048,3,512]{2,0,1:T(8,128)(2,1)} async-done(((bf16[64,3,512]{2,0,1:T(8,128)(2,1)}), bf16[2048,3,512]{2,0,1:T(8,128)(2,1)}) %all-gather.5.cloned.1.call-update) | async-done | bytes 6291472 | tf_op jit(solution)/shard_map/all_gather | solution.py:139
  190.6 8.9 copy.101
  199.5 8.5 convolution_add_fusion
  208.0 3.6 copy.102
  211.6 5.2 reshape.1037
  220.0 6.6 all-to-all-start
  231.1 4.6 all-to-all-done
  235.7 8.9 all-to-all-start.2
  247.5 6.1 all-to-all-done.2
  253.6 8.0 all-to-all-start.1
  299.9 3.6 copy.109
  303.6 3.8 reshape.1071
  307.4 7.2 all-to-all-start.3
  314.7 3.2 fusion.79
  317.9 4.1 fusion.54
  322.0 5.7 fusion.60
  331.6 3.7 multiply_reduce_fusion.2
  352.0 7.6 all-to-all-start.7
  361.3 3.6 copy.114
  364.9 3.8 reshape.1077
  371.0 7.2 all-to-all-start.5
  378.2 2.8 fusion.42
  387.9 7.3 all-to-all-start.6
  397.3 3.0 reshape.1072
  404.0 3.0 reshape.1074
  411.4 3.0 reshape.1078
  419.7 3.0 reshape.1076
  429.5 11.9 fusion.111
  445.6 8.7 fusion.117
  454.6 4.3 convolution_convert_fusion.5
  458.9 10.6 fusion.116
  469.6 11.1 convolution_convert_fusion.4
  480.7 11.7 fusion.109
  493.8 5.8 add_convert_fusion.1
  499.7 8.2 convolution_convert_fusion.2
  508.0 10.9 convolution_convert_fusion
  519.1 10.1 convolution_convert_fusion.1
  531.4 76.3 %reduce-scatter.7.cloned.1.call-done = bf16[512,64]{0,1:T(8,128)(2,1)} async-done(((bf16[512,2048]{0,1:T(8,128)(2,1)}), bf16[512,64]{0,1:T(8,128)(2,1)}) %reduce-scatter.7.cloned.1.call-update) | async-done | bytes 65552 | tf_op jit(solution)/shard_map/reduce_scatter | solution.py:241
  609.2 127.9 %all-reduce.6.cloned.1.call-done = (bf16[512,2048]{1,0:T(8,128)(2,1)}, bf16[512,2048]{1,0:T(8,128)(2,1)}, bf16[512,2048]{1,0:T(8,128)(2,1)}) async-done(((bf16[512,2048]{1,0:T(8,128)(2,1)}, bf16[512,2048]{1,0:T(8,128)(2,1)}, bf16[512,2048]{1,0:T(8,128)(2,1)}), (bf16[512,2048]{1,0:T(8,128)(2,1)}, bf16[512,2048]{1,0:T(8,128)(2,1)}, bf16[512,2048]{1,0:T(8,128)(2,1)})) %all-reduce.6.cloned.1.call-update) | async-done | bytes 6291472 | tf_op jit(solution)/shard_map/psum | solution.py:171
  739.1 2.7 fusion.6
  743.9 146.3 %all-reduce.2 = (bf16[2048]{0:T(1024)(128)(2,1)S(1)}, bf16[2048]{0:T(1024)(128)(2,1)S(1)}, bf16[3,512]{1,0:T(4,128)(2,1)S(1)}, bf16[2048]{0:T(1024)(128)(2,1)S(1)}, bf16[2048]{0:T(1024)(128)(2,1)S(1)}) all-reduce(bf16[2048]{0:T(1024)(128)(2,1)S(1)} %get-tuple-element.124, ...), channel_id=1, replica_groups=mesh['fsdp'=4,'sp'=8,'tp'=4] {'fsdp','sp'}, use_global_device_ids=true, to_apply=%region_20.21 | all-reduce | flops 9728 | bytes 38912 | tf_op jit(solution)/shard_map/psum | solution.py:231
  892.7 6.6 add_convert_fusion
  899.2 3.9 reduce-scatter.5.cloned.1.call-done
  904.9 167.1 %reduce-scatter.11.cloned.1.call-done = bf16[2048,64]{0,1:T(8,128)(2,1)} async-done(((bf16[2048,2048]{0,1:T(8,128)(2,1)}), bf16[2048,64]{0,1:T(8,128)(2,1)}) %reduce-scatter.11.cloned.1.call-update) | async-done | bytes 262160 | tf_op jit(solution)/shard_map/reduce_scatter | solution.py:247
  1073.7 168.6 %reduce-scatter.9.cloned.1.call-done = bf16[64,2048]{1,0:T(8,128)(2,1)} async-done(((bf16[2048,2048]{1,0:T(8,128)(2,1)}), bf16[64,2048]{1,0:T(8,128)(2,1)}) %reduce-scatter.9.cloned.1.call-update) | async-done | bytes 262160 | tf_op jit(solution)/shard_map/reduce_scatter | solution.py:244
  (291 shorter events, 137.6 us)
Async XLA Ops:
  7.2 6.2 copy-start.1
  7.2 7.5 copy-start.58
  7.2 7.5 copy-start.59
  7.2 8.1 copy-start.60
  7.2 8.1 copy-start.61
  7.2 86.2 %all-gather.7.cloned.1.call-start = ((), (), s32[]{:S(2)}) async-start(), calls=%async_computation.13 | async-start | bytes 2162688 | tf_op jit(solution)/shard_map/all_gather | solution.py:140
  8.0 182.7 %all-gather.5.cloned.1.call-start = ((), (), s32[]{:S(2)}) async-start(), calls=%async_computation.12 | async-start | bytes 6488064 | tf_op jit(solution)/shard_map/all_gather | solution.py:139
  8.7 450.2 %all-gather.9.cloned.1.call-start = ((), (), s32[]{:S(2)}) async-start(), calls=%async_computation.14 | async-start | bytes 8650752 | tf_op jit(solution)/shard_map/all_gather | solution.py:141
  9.4 460.1 %all-gather.11.cloned.1.call-start = ((), (), s32[]{:S(2)}) async-start(), calls=%async_computation.15 | async-start | bytes 8650752 | tf_op jit(solution)/shard_map/all_gather | solution.py:142
  17.4 211.6 %copy-start.37 = (f32[256,16]{0,1:T(8,128)}, f32[256,16]{0,1:T(8,128)S(1)}, u32[]{:S(2)}) copy-start(f32[256,16]{0,1:T(8,128)S(1)} %get-tuple-element.160) | copy-start | bytes 49156
  98.0 121.2 %all-to-all-start.4 = ((bf16[2,256,8,64]{1,0,3,2:T(2,128)(2,1)}), bf16[2,256,8,64]{1,0,3,2:T(2,128)(2,1)S(1)}, u32[]{:S(2)}, u32[]{:S(2)}) async-start(bf16[2,256,8,64]{1,0,3,2:T(2,128)(2,1)} %reshape.1053), calls=%async_computation.4 | async-start | bytes 1048576 | tf_op jit(solution)/shard_map/all_to_all | solution.py:195
  220.0 15.7 %all-to-all-start = ((bf16[2,256,8,64]{1,0,3,2:T(2,128)(2,1)}), bf16[2,256,8,64]{1,0,3,2:T(2,128)(2,1)}, u32[]{:S(2)}, u32[]{:S(2)}) async-start(bf16[2,256,8,64]{1,0,3,2:T(2,128)(2,1)} %fusion.100), calls=%async_computation | async-start | bytes 1048576 | tf_op jit(solution)/shard_map/all_to_all | solution.py:166
  235.7 17.9 %all-to-all-start.2 = ((bf16[2,256,8,64]{1,0,3,2:T(2,128)(2,1)}), bf16[2,256,8,64]{1,0,3,2:T(2,128)(2,1)}, u32[]{:S(2)}, u32[]{:S(2)}) async-start(bf16[2,256,8,64]{1,0,3,2:T(2,128)(2,1)} %pad_maximum_fusion.1), calls=%async_computation.2 | async-start | bytes 1048576 | tf_op jit(solution)/shard_map/all_to_all | solution.py:165
  253.6 18.3 %all-to-all-start.1 = ((bf16[2,256,8,64]{1,0,3,2:T(2,128)(2,1)}), bf16[2,256,8,64]{1,0,3,2:T(2,128)(2,1)}, u32[]{:S(2)}, u32[]{:S(2)}) async-start(bf16[2,256,8,64]{1,0,3,2:T(2,128)(2,1)} %pad_maximum_fusion), calls=%async_computation.1 | async-start | bytes 1048576 | tf_op jit(solution)/shard_map/all_to_all | solution.py:164
  264.8 12.9 %copy-start.15 = (bf16[2,2048,1,64]{1,3,0,2:T(8,128)(2,1)}, bf16[2,2048,1,64]{1,3,0,2:T(8,128)(2,1)S(1)}, u32[]{:S(2)}) copy-start(bf16[2,2048,1,64]{1,3,0,2:T(8,128)(2,1)S(1)} %all_to_all.102) | copy-start | bytes 1572868
  264.8 10.5 copy-start.36
  283.6 10.4 copy-start.3
  283.6 10.4 copy-start.53
  284.8 9.3 copy-start.55
  288.0 7.2 copy-start.2
  288.0 7.2 copy-start.49
  299.9 14.6 %copy-start.54 = (f32[2,512]{1,0:T(2,128)S(1)}, f32[2,512]{1,0:T(2,128)}, u32[]{:S(2)}) copy-start(f32[2,512]{1,0:T(2,128)} %copy-done.53) | copy-start | bytes 12292
  299.9 14.6 %copy-start.56 = (f32[2,512]{1,0:T(2,128)S(1)}, f32[2,512]{1,0:T(2,128)}, u32[]{:S(2)}) copy-start(f32[2,512]{1,0:T(2,128)} %copy-done.55) | copy-start | bytes 12292
  299.9 14.7 %copy-start.50 = (f32[2,512]{1,0:T(2,128)S(1)}, f32[2,512]{1,0:T(2,128)}, u32[]{:S(2)}) copy-start(f32[2,512]{1,0:T(2,128)} %copy-done.49) | copy-start | bytes 12292
  299.9 14.7 %copy-start.52 = (f32[2,512]{1,0:T(2,128)S(1)}, f32[2,512]{1,0:T(2,128)}, u32[]{:S(2)}) copy-start(f32[2,512]{1,0:T(2,128)} %copy-done.51) | copy-start | bytes 12292
  299.9 14.7 %copy-start.46 = (f32[2,512]{1,0:T(2,128)S(1)}, f32[2,512]{1,0:T(2,128)}, u32[]{:S(2)}) copy-start(f32[2,512]{1,0:T(2,128)} %copy-done.45) | copy-start | bytes 12292
  299.9 14.7 %copy-start.48 = (f32[2,512]{1,0:T(2,128)S(1)}, f32[2,512]{1,0:T(2,128)}, u32[]{:S(2)}) copy-start(f32[2,512]{1,0:T(2,128)} %copy-done.47) | copy-start | bytes 12292
  307.4 44.6 %all-to-all-start.3 = ((bf16[8,2,16384]{2,1,0:T(2,128)(2,1)}), bf16[8,2,16384]{2,1,0:T(2,128)(2,1)}, u32[]{:S(2)}, u32[]{:S(2)}) async-start(bf16[8,2,16384]{2,1,0:T(2,128)(2,1)} %reshape.1071), calls=%async_computation.3 | async-start | bytes 1048576 | tf_op jit(solution)/shard_map/all_to_all | solution.py:173
  349.9 18.8 %copy-start.10 = (f32[2,2048,1,64]{1,3,0,2:T(8,128)S(1)}, f32[2,2048,1,64]{1,3,0,2:T(8,128)}, u32[]{:S(2)}) copy-start(f32[2,2048,1,64]{1,3,0,2:T(8,128)} %scatter-add.20) | copy-start | bytes 3145732
  352.0 19.0 %all-to-all-start.7 = ((bf16[8,2,16384]{2,1,0:T(2,128)(2,1)}), bf16[8,2,16384]{2,1,0:T(2,128)(2,1)}, u32[]{:S(2)}, u32[]{:S(2)}) async-start(bf16[8,2,16384]{2,1,0:T(2,128)(2,1)} %reshape.1073), calls=%async_computation.7 | async-start | bytes 1048576 | tf_op jit(solution)/shard_map/all_to_all | solution.py:208
  371.0 16.9 %all-to-all-start.5 = ((bf16[8,2,16384]{2,1,0:T(2,128)(2,1)}), bf16[8,2,16384]{2,1,0:T(2,128)(2,1)}, u32[]{:S(2)}, u32[]{:S(2)}) async-start(bf16[8,2,16384]{2,1,0:T(2,128)(2,1)} %reshape.1077), calls=%async_computation.5 | async-start | bytes 1048576 | tf_op jit(solution)/shard_map/all_to_all | solution.py:206
  381.4 13.7 %copy-start.40 = (f32[1,2,2,128]{3,1,2,0:T(2,128)S(1)}, f32[1,2,2,128]{3,1,2,0:T(2,128)}, u32[]{:S(2)}) copy-start(f32[1,2,2,128]{3,1,2,0:T(2,128)} %copy.133) | copy-start | bytes 6148
  381.4 13.7 %copy-start.41 = (f32[512]{0:T(512)S(1)}, f32[512]{0:T(512)}, u32[]{:S(2)}) copy-start(f32[512]{0:T(512)} %rsqrt.15) | copy-start | bytes 6148
  387.9 31.8 %all-to-all-start.6 = ((bf16[8,2,16384]{2,1,0:T(2,128)(2,1)}), bf16[8,2,16384]{2,1,0:T(2,128)(2,1)}, u32[]{:S(2)}, u32[]{:S(2)}) async-start(bf16[8,2,16384]{2,1,0:T(2,128)(2,1)} %reshape.1075), calls=%async_computation.6 | async-start | bytes 1048576 | tf_op jit(solution)/shard_map/all_to_all | solution.py:207
  395.1 212.5 %reduce-scatter.7.cloned.1.call-start = ((), (), s32[]{:S(2)}) async-start(), calls=%async_computation.17 | async-start | bytes 2162688 | tf_op jit(solution)/shard_map/reduce_scatter | solution.py:241
  428.0 14.9 %copy-start.13 = (bf16[2,256,2048]{2,1,0:T(8,128)(2,1)S(1)}, bf16[2,256,2048]{2,1,0:T(8,128)(2,1)}, u32[]{:S(2)}) copy-start(bf16[2,256,2048]{2,1,0:T(8,128)(2,1)} %param.43) | copy-start | bytes 6291460
  428.0 14.9 %copy-start.34 = (bf16[64,8,2,256]{3,1,2,0:T(8,128)(2,1)S(1)}, bf16[64,8,2,256]{3,1,2,0:T(8,128)(2,1)}, u32[]{:S(2)}) copy-start(bf16[64,8,2,256]{3,1,2,0:T(8,128)(2,1)} %copy.132) | copy-start | bytes 1572868
  454.3 282.7 %all-reduce.6.cloned.1.call-start = ((), (), s32[]{:S(2)}) async-start(), calls=%async_computation.20 | async-start | bytes 12582912 | tf_op jit(solution)/shard_map/psum | solution.py:171
  458.9 10.6 copy-start.57
  469.5 11.1 copy-start.14
  469.6 24.2 %slice-start.4 = ((s8[8388608]{0:T(1024)(128)(4,1)}), s8[4194304]{0:T(1024)(128)(4,1)S(1)}, s32[]{:S(2)}) async-start(s8[8388608]{0:T(1024)(128)(4,1)} %bitcast.405), calls=%async_computation.25 | async-start | bytes 8388608
  480.7 13.1 %slice-start.5 = ((s8[8388608]{0:T(1024)(128)(4,1)}), s8[4194304]{0:T(1024)(128)(4,1)S(1)}, s32[]{:S(2)}) async-start(s8[8388608]{0:T(1024)(128)(4,1)} %bitcast.405), calls=%async_computation.26 | async-start | bytes 8388608
  480.7 13.1 %copy-start.64 = (f32[512,2048]{1,0:T(8,128)S(1)}, f32[512,2048]{1,0:T(8,128)}, u32[]{:S(2)}) copy-start(f32[512,2048]{1,0:T(8,128)} %fusion.117) | copy-start | bytes 12582916
  499.6 403.5 %reduce-scatter.5.cloned.1.call-start = ((), (), s32[]{:S(2)}) async-start(), calls=%async_computation.16 | async-start | bytes 6488064 | tf_op jit(solution)/shard_map/reduce_scatter | solution.py:238
  507.9 564.0 %reduce-scatter.11.cloned.1.call-start = ((), (), s32[]{:S(2)}) async-start(), calls=%async_computation.19 | async-start | bytes 8650752 | tf_op jit(solution)/shard_map/reduce_scatter | solution.py:247
  518.9 723.5 %reduce-scatter.9.cloned.1.call-start = ((), (), s32[]{:S(2)}) async-start(), calls=%async_computation.18 | async-start | bytes 8650752 | tf_op jit(solution)/shard_map/reduce_scatter | solution.py:244
  529.3 212.5 %copy-start.44 = (f32[1,2,2,128]{3,1,2,0:T(2,128)S(1)}, f32[1,2,2,128]{3,1,2,0:T(2,128)}, u32[]{:S(2)}) copy-start(f32[1,2,2,128]{3,1,2,0:T(2,128)} %copy-done.43) | copy-start | bytes 6148
  890.9 353.3 %copy-start.42 = (f32[2048]{0:T(1024)}, f32[2048]{0:T(1024)S(1)}, u32[]{:S(2)}) copy-start(f32[2048]{0:T(1024)S(1)} %convert_element_type.370) | copy-start | bytes 24580
  (41 other events, 118.2 us)
Sparse Core Ops, SparseCore 0:
  9.7 83.6 all-gather.6
  95.1 95.4 all-gather.4
  192.3 103.9 all-gather.8
  297.8 105.3 all-gather.10
  454.5 153.1 reduce-scatter.6
  610.8 126.2 all-reduce.5
  739.6 163.4 reduce-scatter.4
  905.7 166.2 reduce-scatter.10
  1074.5 167.8 reduce-scatter.8
where the time goes:
time: 1260 us; the launch traced here: 1250 us
  waiting for transfers between devices  716 us (57%)
  blocking collectives  146 us (12%)
  matrix products  144 us (11%)
  local copies, waits for them, and re-layouts  100 us (8%)
  other arithmetic  68.9 us (5%)
  starting transfers between devices  60.9 us (5%)
  between operations  15.2 us (1%)
    reduce_scatter x1, waiting for transfers between devices, body(): lax.psum_scatter(grad_w_fc1.astype(jnp.bfloat16), ('fsdp', 'sp'), scatter...  169 us
    reduce_scatter x1, waiting for transfers between devices, body(): lax.psum_scatter(grad_w_fc2.astype(jnp.bfloat16), ('fsdp', 'sp'), scatter...  167 us
    psum x1, blocking collectives, body(): lax.psum(grad_gain_local.astype(jnp.bfloat16), ('fsdp', 'sp'))  146 us
    psum x1, waiting for transfers between devices, body(): lax.psum(mlp_part.astype(jnp.bfloat16), 'tp').astype(jnp.float32)  128 us
    all_gather x1, waiting for transfers between devices, body(): lax.all_gather(w_qkv, ('fsdp', 'sp'), axis=0, tiled=True)  85.1 us
    reduce_scatter x1, waiting for transfers between devices, body(): lax.psum_scatter(grad_w_dense.astype(jnp.bfloat16), ('fsdp', 'sp'), scatt...  76.3 us
    all_gather x1, waiting for transfers between devices, body(): lax.all_gather(w_dense, ('fsdp', 'sp'), axis=1, tiled=True)  73.8 us
    unnamed x160, local copies, waits for them, and re-layouts  39.7 us
  transfers between devices with their start and end apart: 17, of which 9 were waited for; matrix products, arithmetic and copies ran while one was open for 24% of the time, Pallas kernels for 0%

commit v1 on v0

v1 whole, which is shorter than its diff:
```python
import functools
import math

import jax
import jax.numpy as jnp
from jax import lax
from jax.experimental import pallas as pl
from jax.experimental.pallas import tpu as pltpu
from jax.sharding import PartitionSpec as P

MESH = pl.DeviceIdType.MESH
F32 = jnp.float32
BF = jnp.bfloat16
HDIM = 64
ROT = 32
TQ = 512
LOG2E = 1.4426950408889634
MIB = 2**20


def dot_nt(a, b):
    return lax.dot_general(a, b, (((1,), (1,)), ((), ())), preferred_element_type=F32)


def dot_nn(a, b):
    return lax.dot_general(a, b, (((1,), (0,)), ((), ())), preferred_element_type=F32)


class Scratch:
    def __init__(self, names, refs):
        for name, ref in zip(names, refs):
            setattr(self, name, ref)


class Place:
    def __init__(self):
        f, s, t = (lax.axis_index(a) for a in ("fsdp", "sp", "tp"))
        self.f, self.s = f, s
        self.x, self.y, self.c, self.z = s % 4, (s // 4) * 2 + f // 2, f % 2, t
        self.a1 = self.x * (1 - self.c) + self.y * self.c
        self.a2 = self.y * (1 - self.c) + self.x * self.c

    def xy(self, d1, d2):
        p1, p2, c = (self.a1 + d1 + 4) % 4, (self.a2 + d2 + 4) % 4, self.c
        return p1 * (1 - c) + p2 * c, p2 * (1 - c) + p1 * c

    def dev(self, x, y, c, z):
        return ((y % 2) * 2 + c, (y // 2) * 4 + x, z)

    def peer(self, d1, d2):
        x, y = self.xy(d1, d2)
        return self.dev(x, y, self.c, self.z)

    def sibling(self):
        return self.dev(self.x, self.y, 1 - self.c, self.z)

    def blk(self, d1, d2):
        x, y = self.xy(d1, d2)
        return ((y % 2) * 2 + self.c) * 8 + (y // 2) * 4 + x

    def zpeer(self, d):
        return self.dev(self.x, self.y, self.c, (self.z + d + 4) % 4)

    def sp_peer(self, k):
        return (self.f, (self.s + k) % 8, self.z)


def barrier(devices):
    sem = pltpu.get_barrier_semaphore()
    for d in devices:
        pl.semaphore_signal(sem, inc=1, device_id=d, device_id_type=MESH)
    pl.semaphore_wait(sem, len(devices))


def remote(src, dst, send, recv, device):
    pltpu.make_async_remote_copy(
        src_ref=src, dst_ref=dst, send_sem=send, recv_sem=recv, device_id=device, device_id_type=MESH
    ).start()


def wait_bytes(ref, sem):
    pltpu.make_async_copy(ref, ref, sem).wait()


STEP = (0, -1, 1, 2)


class Gather:
    def __init__(self, p, shard, w, send, recv, local):
        self.p, self.shard, self.w, self.send, self.recv, self.local = p, shard, w, send, recv, local

    def push(self, b, sem, device, half=None, src=None):
        dst = self.w.at[b] if half is None else self.w.at[b, pl.ds(32 * half, 32)]
        remote(dst if src is None else src, dst, self.send, self.recv.at[sem], device)

    def arrive(self, b, sem):
        wait_bytes(self.w.at[b], self.recv.at[sem])

    def start(self):
        p, s = self.p, self.shard
        own = p.blk(0, 0)
        for sem, device in ((0, p.peer(1, 0)), (1, p.peer(-1, 0)), (3, p.peer(0, 1)), (7, p.peer(0, -1)), (15, p.sibling())):
            self.push(own, sem, device, src=s)
        pltpu.make_async_copy(s, self.w.at[own], self.local).start()

    def second(self, j):
        p = self.p
        b = p.blk(STEP[j], 0)
        self.push(b, 3 + j, p.peer(0, 1))
        self.push(b, 7 + j, p.peer(0, -1))
        self.push(b, 15, p.sibling())

    def first_low(self):
        p = self.p
        b = p.blk(-1, 0)
        self.arrive(b, 0)
        self.push(b, 2, p.peer(1, 0), half=0)
        self.second(1)

    def first_high(self):
        p = self.p
        b = p.blk(1, 0)
        self.arrive(b, 1)
        self.push(b, 2, p.peer(-1, 0), half=1)
        self.second(2)

    def first_far(self):
        self.arrive(self.p.blk(2, 0), 2)
        self.second(3)

    def low(self, j):
        p = self.p
        b = p.blk(STEP[j], -1)
        self.arrive(b, 3 + j)
        self.push(b, 11 + j, p.peer(0, 1), half=0)
        self.push(b, 15, p.sibling())

    def high(self, j):
        p = self.p
        b = p.blk(STEP[j], 1)
        self.arrive(b, 7 + j)
        self.push(b, 11 + j, p.peer(0, -1), half=1)
        self.push(b, 15, p.sibling())

    def far(self, j):
        b = self.p.blk(STEP[j], 2)
        self.arrive(b, 11 + j)
        self.push(b, 15, self.p.sibling())

    def end(self):
        wait_bytes(self.w.at[pl.ds(0, 16)], self.recv.at[15])
        own = self.p.blk(0, 0)
        pltpu.make_async_copy(self.shard, self.w.at[own], self.local).wait()

    def drain(self):
        wait_bytes(self.w.at[pl.ds(0, 31)], self.send)

    def ticks(self):
        part = functools.partial
        return [
            self.first_low, self.first_high, part(self.low, 0), part(self.high, 0), self.first_far,
            part(self.low, 1), part(self.high, 1), part(self.far, 0), part(self.low, 2), part(self.high, 2), part(self.far, 1),
            part(self.low, 3), part(self.high, 3), part(self.far, 2), part(self.far, 3), self.end,
        ]


class Ticks:
    def __init__(self):
        self.todo = []

    def add(self, key, fn):
        self.todo.append((key, len(self.todo), fn))
        self.todo.sort(key=lambda e: e[:2])

    def run(self, count=1):
        for _ in range(min(count, len(self.todo))):
            self.todo.pop(0)[2]()

    def until(self, fn):
        while any(e[2] == fn for e in self.todo):
            self.run()


ATT = dict(
    q=((2048, 64), BF), k=((2048, 64), BF), v=((2048, 64), BF), g=((2048, 64), BF),
    kt=((64, 2048), BF), vt=((80, 2048), BF), gt=((64, 2048), F32),
    dkv=((2048, 128), F32), mx=((8, TQ), F32), st=((4, TQ, TQ), F32), e=((4, TQ, TQ), BF),
    ot=((80, TQ), F32), dq=((64, TQ), F32), g2=((TQ, 64), BF),
)


def split_heads(recv, seq, b):
    @pl.loop(0, 8)
    def _(i):
        part = recv[i, pl.ds(seq * 256, 256), :]
        rows = pl.ds(i * 256, 256)
        q, k, v, g = (part[:, 64 * n : 64 * n + 64] for n in range(4))
        b.q[rows, :] = q
        b.k[rows, :] = k
        b.v[rows, :] = v
        b.g[rows, :] = g
        cols = pl.ds(pl.multiple_of(i * 256, 256), 256)
        b.kt[:, cols] = k.astype(F32).T.astype(BF)
        b.vt[0:64, cols] = v.astype(F32).T.astype(BF)
        b.gt[:, cols] = g.astype(F32).T

    b.vt[64:80, :] = jnp.ones((16, 2048), BF)
    b.dkv[...] = jnp.zeros(b.dkv.shape, F32)


def attend_block(qi, seq, b, send, tick):
    scale = 0.125 * LOG2E
    qrows = slice(qi * TQ, (qi + 1) * TQ)
    q = b.q[qrows, :]
    b.mx[...] = jnp.full((8, TQ), -1e30, F32)

    def scores(j, masked):
        st = dot_nt(b.k[pl.ds(j * TQ, TQ), :], q)
        if masked:
            key = lax.broadcasted_iota(jnp.int32, (TQ, TQ), 0)
            query = lax.broadcasted_iota(jnp.int32, (TQ, TQ), 1)
            st = jnp.where(key <= query, st, -1e30)
        b.st[j] = st
        b.mx[...] = jnp.maximum(b.mx[...], jnp.max(st.reshape(TQ // 8, 8, TQ), axis=0))

    if qi > 0:

        @pl.loop(0, qi)
        def _(j):
            scores(j, False)

    scores(qi, True)
    top = jnp.max(b.mx[...], axis=0, keepdims=True) * scale
    tick()
    b.ot[...] = jnp.zeros(b.ot.shape, F32)

    @pl.loop(0, qi + 1)
    def _(j):
        e = jnp.exp2(b.st[j] * scale - top).astype(BF)
        b.e[j] = e
        b.ot[...] += dot_nn(b.vt[:, pl.ds(pl.multiple_of(j * TQ, TQ), TQ)], e)

    inv = 1.0 / b.ot[64:65, :]
    out = b.ot[0:64, :] * inv
    gt = b.gt[:, qrows] * inv
    inner = jnp.sum(out * gt, axis=0, keepdims=True)
    b.g2[...] = gt.T.astype(BF)
    tick()
    b.dq[...] = jnp.zeros(b.dq.shape, F32)

    @pl.loop(0, qi + 1)
    def _(j):
        rows = pl.ds(j * TQ, TQ)
        g2 = b.g2[...]
        dp = dot_nt(b.v[rows, :], g2)
        e = b.e[j]
        ds = (e.astype(F32) * (dp - inner)).astype(BF)
        b.dkv[rows, 0:64] += dot_nn(ds, b.q[qrows, :])
        b.dkv[rows, 64:128] += dot_nn(e, g2)
        b.dq[...] += dot_nn(b.kt[:, pl.ds(pl.multiple_of(j * TQ, TQ), TQ)], ds)

    both = jnp.concatenate([out, b.dq[...] * 0.125], axis=0).T.astype(BF)
    for h in range(2):
        send[qi * 2 + h, seq * 256 : (seq + 1) * 256, 0:128] = both[h * 256 : (h + 1) * 256]
    tick()


def finish_heads(seq, b, send):
    @pl.loop(0, 8)
    def _(i):
        t = b.dkv[pl.ds(i * 256, 256), :]
        lane = lax.broadcasted_iota(jnp.int32, t.shape, 1)
        send[i, pl.ds(seq * 256, 256), 128:256] = (t * jnp.where(lane < 64, 0.125, 1.0)).astype(BF)


def turn(a, cos, low, high):
    return a * cos + pltpu.roll(a, 112, 1) * low + pltpu.roll(a, 16, 1) * high


K1 = dict(
    wa=((32, 64, 2048), BF), wb=((32, 64, 2048), BF), wc=((32, 64, 2048), BF),
    hid=((512, 2048), BF), gv=((512, 2048), BF), act=((512, 2048), BF), din=((512, 2048), BF),
    hs=((8, 512, 256), BF), hr=((8, 512, 256), BF), br=((8, 512, 256), BF), gp=((512, 2048), F32),
    dproj=((512, 1536), BF), att=((512, 512), BF), sums=((8, 2048), F32),
)


def block_kernel(
    x_hbm, g_hbm, sa, sb, sc, gain, shift, bqkv, bfc1, cos, low, high,
    o_hid, o_act, o_din, o_dproj, o_att, o_norm, o_mixed, o_sums, *refs,
):
    names = list(K1) + list(ATT)
    m = Scratch(names, refs[: len(names)])
    wsend, wrecv, wlocal, asend, arecv, local, lout = refs[len(names) :]
    p = Place()
    barrier([p.sp_peer(k) for k in range(1, 8)] + [p.dev(p.x, (p.y + k) % 4, p.c, p.z) for k in (1, 3)] + [p.sibling()])
    ga, gb, gc = (
        Gather(p, s, w, wsend.at[i], wrecv.at[i], wlocal.at[i]) for i, (s, w) in enumerate(((sa, m.wa), (sb, m.wb), (sc, m.wc)))
    )
    ga.start()
    gb.start()
    load_x = pltpu.make_async_copy(x_hbm, m.act, local.at[0])
    load_g = pltpu.make_async_copy(g_hbm, m.gv, local.at[1])
    load_x.start()
    load_g.start()
    ticks = Ticks()
    for i, g in enumerate((ga, gb)):
        for k, t in enumerate(g.ticks()):
            ticks.add(i * 9 + k, t)

    load_x.wait()

    def norm_rows(n):
        @pl.loop(0, 4)
        def _(r):
            rows = pl.ds(n * 128 + r * 32, 32)
            x = m.act[rows, :].astype(F32)
            cent = x - jnp.mean(x, axis=-1, keepdims=True)
            inv = lax.rsqrt(jnp.mean(cent * cent, axis=-1, keepdims=True) + 1e-05)
            m.hid[rows, :] = (cent * inv * gain[...] + shift[...]).astype(BF)

    for n in range(4):
        norm_rows(n)
        if n > 1:
            ticks.run()
    outs = []

    def put(src, dst):
        c = pltpu.make_async_copy(src, dst, lout.at[len(outs)])
        c.start()
        outs.append(c)

    put(m.hid, o_hid)
    load_g.wait()

    @pl.loop(0, 8)
    def _(n):
        cols = pl.ds(pl.multiple_of(n * 256, 256), 256)
        m.sums[2:3, cols] = jnp.sum(m.gv[:, cols].astype(F32), axis=0, keepdims=True)

    ticks.until(ga.end)

    for part in range(4):
        for t in range(2):
            col = part * 512 + t * 256
            lhs = m.gv if part == 3 else m.hid
            acc = dot_nn(lhs[...], m.wa[:, :, col : col + 256].reshape(2048, 256))
            if part < 3:
                acc = acc + bqkv[:, col : col + 256]
            for sq in range(2):
                for lh in range(2):
                    a = acc[sq * 256 : (sq + 1) * 256, lh * 128 : (lh + 1) * 128]
                    if part < 2:
                        a = turn(a, cos[...], low[...], high[...])
                    a = a.astype(BF)
                    for e in range(2):
                        m.hs[t * 4 + lh * 2 + e, sq * 256 : (sq + 1) * 256, part * 64 : part * 64 + 64] = a[:, e * 64 : e * 64 + 64]
            if t:
                ticks.run()

    def exchange(dst, recv, seq, base):
        rows = pl.ds(seq * 256, 256)
        for k in range(1, 8):
            to = (p.s + k) % 8
            remote(m.hs.at[to, rows], dst.at[p.s, rows], asend.at[base], recv, p.sp_peer(k))
        c = pltpu.make_async_copy(m.hs.at[p.s, rows], dst.at[p.s, rows], local.at[2 + base])
        c.start()
        return c

    def exchanged(dst, recv, seq, own):
        wait_bytes(dst.at[pl.ds(0, 7), pl.ds(seq * 256, 256)], recv)
        own.wait()

    def sent(base):
        wait_bytes(m.hs.at[pl.ds(0, 7), pl.ds(0, 256)], asend.at[base])

    own = [exchange(m.hr, arecv.at[seq], seq, seq) for seq in range(2)]
    gc.start()
    for k, t in enumerate(gc.ticks()):
        ticks.add(19 + k, t)
    ticks.until(gb.end)

    def hidden_units(n):
        cols = slice(n * 256, n * 256 + 256)
        u = dot_nn(m.hid[...], m.wb[:, :, cols].reshape(2048, 256)) + bfc1[:, cols]
        k = math.sqrt(2.0 / math.pi)
        sq = u * u
        th = jnp.tanh(u * (k + (k * 0.044715) * sq))
        half = 0.5 + 0.5 * th
        m.act[:, cols] = (u * half).astype(BF)
        m.gp[:, cols] = half + (0.5 * u) * (1.0 - th * th) * (k + (3.0 * k * 0.044715) * sq)

    for n in range(8):
        hidden_units(n)
        if n % 2:
            ticks.run()
    put(m.act, o_act)

    back = []
    for seq in range(2):
        exchanged(m.hr, arecv.at[seq], seq, own[seq])
        split_heads(m.hr, seq, m)
        if seq == 0:
            sent(0)
            sent(1)
        for qi in range(4):
            attend_block(qi, seq, m, m.hs, ticks.run)
        finish_heads(seq, m, m.hs)
        back.append(exchange(m.br, arecv.at[2 + seq], seq, 2 + seq))
    ticks.until(gc.end)

    for n in range(8):
        cols = slice(n * 256, n * 256 + 256)
        ga_ = dot_nn(m.gv[...], m.wc[:, :, cols].reshape(2048, 256))
        d = (ga_ * m.gp[:, cols]).astype(BF)
        m.din[:, cols] = d
        m.sums[0:1, cols] = jnp.sum(d.astype(F32), axis=0, keepdims=True)
    put(m.din, o_din)

    @pl.loop(0, 4)
    def _(t):
        rows = pl.ds(t * 8, 8)
        cols = pl.ds(pl.multiple_of(t * 512, 512), 512)
        m.gp[:, cols] = dot_nt(m.act[...], m.wc[rows].reshape(512, 2048))
        m.st[t] = dot_nt(m.din[...], m.wb[rows].reshape(512, 2048))

    for seq in range(2):
        exchanged(m.br, arecv.at[2 + seq], seq, back[seq])

    for hp in range(4):
        pair = [m.br[2 * hp + e] for e in range(2)]
        for n in range(4):
            a = jnp.concatenate([pair[e][:, n * 64 : n * 64 + 64] for e in range(2)], axis=1)
            cols = slice(hp * 128, hp * 128 + 128)
            if n == 0:
                m.att[:, cols] = a
                continue
            if n < 3:
                a = a.astype(F32)
                a = jnp.concatenate(
                    [turn(a[sq * 256 : sq * 256 + 256], cos[...], -low[...], -high[...]) for sq in range(2)], axis=0
                ).astype(BF)
            cols = slice((n - 1) * 512 + hp * 128, (n - 1) * 512 + hp * 128 + 128)
            m.dproj[:, cols] = a
            m.sums[1:2, cols] = jnp.sum(a.astype(F32), axis=0, keepdims=True)
    put(m.att, o_att)
    put(m.dproj, o_dproj)
    outs[0].wait()

    @pl.loop(0, 4)
    def _(t):
        rows = pl.ds(t * 8, 8)
        cols = pl.ds(pl.multiple_of(t * 512, 512), 512)
        norm = m.st[t] + dot_nt(m.dproj[...], m.wa[rows, :, 0:1536].reshape(512, 1536))
        m.hid[:, cols] = norm.astype(BF)
        mixed = m.gp[:, cols] + dot_nt(m.att[...], m.wa[rows, :, 1536:2048].reshape(512, 512))
        m.gv[:, cols] = mixed.astype(BF)

    put(m.hid, o_norm)
    put(m.gv, o_mixed)
    put(m.sums, o_sums)
    for g in (ga, gb, gc):
        g.drain()
    sent(2)
    sent(3)
    for c in outs[1:]:
        c.wait()


def run_block(x, g, sa, sb, sc, gain, shift, bqkv, bfc1, cos, low, high):
    hbm = pl.BlockSpec(memory_space=pl.ANY)
    vmem = pl.BlockSpec(memory_space=pltpu.VMEM)
    full = jax.ShapeDtypeStruct((512, 2048), BF)
    dma = pltpu.SemaphoreType.DMA
    return pl.pallas_call(
        block_kernel,
        out_shape=[
            full, full, full, jax.ShapeDtypeStruct((512, 1536), BF), jax.ShapeDtypeStruct((512, 512), BF), full, full,
            jax.ShapeDtypeStruct((8, 2048), F32),
        ],
        in_specs=[hbm] * 5 + [vmem] * 7,
        out_specs=[hbm] * 8,
        scratch_shapes=[pltpu.VMEM(*v) for v in (K1 | ATT).values()]
        + [dma((3,)), dma((3, 16)), dma((3,)), dma((4,)), dma((4,)), dma((6,)), dma((8,))],
        compiler_params=pltpu.CompilerParams(collective_id=0, has_side_effects=True, vmem_limit_bytes=60 * MIB),
        cost_estimate=pl.CostEstimate(flops=30 * 10**9, bytes_accessed=20 * 10**6, transcendentals=10**7),
    )(x, g, sa, sb, sc, gain, shift, bqkv, bfc1, cos, low, high)


def layer_norm(inputs, gain, shift):
    average = jnp.mean(inputs, axis=-1, keepdims=True)
    centered = inputs - average
    spread = jnp.mean(centered * centered, axis=-1, keepdims=True)
    return centered * lax.rsqrt(spread + 1e-05) * gain + shift


def contract_first(left, right):
    return lax.dot_general(left, right, (((0,), (0,)), ((), ())), preferred_element_type=F32)


def body(tokens, ln_gain, ln_bias, w_qkv, b_qkv, w_dense, b_dense, w_fc1, b_fc1, w_fc2, b_fc2, cotangent):
    seq_count, local_len, width = tokens.shape
    rows = seq_count * local_len
    x = tokens.reshape(rows, width)
    g = cotangent.reshape(rows, width)
    gain = ln_gain.astype(F32)
    shift = ln_bias.astype(F32)
    places = (lax.axis_index("sp") * local_len + jnp.arange(local_len, dtype=jnp.int32)).astype(F32)
    freqs = jnp.exp(jnp.arange(ROT // 2, dtype=F32) * (-2.0 * math.log(10000.0) / ROT))
    angle = places[:, None] * freqs[None, :]
    c, s = jnp.cos(angle), jnp.sin(angle)
    one, zero = jnp.ones((local_len, 32), F32), jnp.zeros((local_len, 16), F32)
    cos = jnp.concatenate([c, c, one] * 2, axis=1)
    low = jnp.concatenate([-s, zero, zero, zero] * 2, axis=1)
    high = jnp.concatenate([zero, s, zero, zero] * 2, axis=1)
    sa = jnp.concatenate([w_qkv.reshape(64, 1536), w_dense.T], axis=1)
    hid, act, din, dproj, att, norm, mixed, sums = run_block(
        x, g, sa, w_fc1, w_fc2.T, gain[None], shift[None], b_qkv.astype(F32).reshape(1, 1536), b_fc1.astype(F32)[None], cos, low, high
    )
    x32 = x.astype(F32)
    mixed_out = (
        (x32 + lax.psum(mixed, "tp").astype(F32) + b_dense.astype(F32) + b_fc2.astype(F32)).astype(BF).reshape(tokens.shape)
    )
    grad_normed = lax.psum(norm, "tp").astype(F32)
    grad_x, grad_gain, grad_shift = jax.vjp(layer_norm, x32, gain, shift)[1](grad_normed)
    grad_tokens = (g.astype(F32) + grad_x).astype(BF).reshape(tokens.shape)
    small = jnp.concatenate([grad_gain, grad_shift, sums[0], sums[2], sums[1, :1536]])
    small = lax.psum(small, ("fsdp", "sp"))
    scatter = functools.partial(lax.psum_scatter, axis_name=("fsdp", "sp"), tiled=True)
    gq = scatter(contract_first(hid, dproj).astype(BF), scatter_dimension=0).astype(F32).reshape(64, 3, 512)
    gd = scatter(contract_first(att, g).astype(BF), scatter_dimension=1).astype(F32)
    g1 = scatter(contract_first(hid, din).astype(BF), scatter_dimension=0).astype(F32)
    g2 = scatter(contract_first(act, g).astype(BF), scatter_dimension=1).astype(F32)
    out = small[6144:8192]
    return (
        mixed_out, grad_tokens, small[:2048], small[2048:4096], gq, small[8192:].reshape(3, 512), gd, out, g1,
        small[4096:6144], g2, out,
    )


def solution(mesh):
    both = ("fsdp", "sp")
    act = P("fsdp", "sp", None)
    in_specs = (
        act, P(), P(), P(both, None, "tp"), P(None, "tp"), P("tp", both), P(), P(both, "tp"), P("tp"), P("tp", both), P(), act,
    )
    out_specs = (
        act, act, P(), P(), P(both, None, "tp"), P(None, "tp"), P("tp", both), P(), P(both, "tp"), P("tp"), P("tp", both), P(),
    )
    return jax.shard_map(body, mesh=mesh, in_specs=in_specs, out_specs=out_specs, check_vma=False)
```

time: 1260 us -> 860 us (0.68)
  waiting for transfers between devices: 716 us -> 462 us
  Pallas kernels: 0 us -> 160 us
  matrix products: 144 us -> 29.2 us
  local copies, waits for them, and re-layouts: 100 us -> 10.9 us
  starting transfers between devices: 60.9 us -> 0.39 us
  other arithmetic: 68.9 us -> 25.9 us
    pallas_call x0 -> x1, Pallas kernels: none -> 160 us  [run_block(): pl.pallas_call(block_kernel, out_shape=[full, full, full, jax.ShapeDtypeS...]
    all_gather x4 -> x0, waiting for transfers between devices: 159 us -> none  [the longest x1 85.1 us: body(): lax.all_gather(w_qkv, ('fsdp', 'sp'), axis=0, tiled=True)]
    dot_general x32 -> x0, matrix products: 112 us -> none  [the longest x4 29.7 us: contract_last(): lax.dot_general(left, right, (((1,), (1,)), ((), ())), preferred_element_...]
    psum x1, waiting for transfers between devices: 128 us -> 59.2 us  [body(): lax.psum(mixed, 'tp').astype(F32)]
    all_to_all x8 -> x0, starting transfers between devices: 60.2 us -> none  [the longest x1 8.9 us: body(): lax.all_to_all(key_part, 'sp', split_axis=2, concat_axis=1, tiled=True)]
    unnamed x160 -> x24, local copies, waits for them, and re-layouts: 39.7 us -> 4.41 us
    reduce_sum x6 -> x0, other arithmetic: 17.6 us -> none  [the longest x1 11.9 us: body(): jnp.sum(grad_projected.astype(jnp.float32), axis=0)]
    all_to_all x12 -> x0, local copies, waits for them, and re-layouts: 17.5 us -> none  [the longest x2 3.41 us: body(): lax.all_to_all(query, 'sp', split_axis=2, concat_axis=1, tiled=True)]
  transfers between devices with their start and end apart: 17 -> 5, of which waited for: 9 -> 4; matrix products, arithmetic and copies ran while one was open for 24% -> 6% of each run, Pallas kernels for 0% -> 0%
where the time goes in v1:
time: 860 us; the launch traced here: 850 us
  waiting for transfers between devices  462 us (54%)
  Pallas kernels  160 us (19%)
  blocking collectives  146 us (17%)
  matrix products  29.2 us (3%)
  other arithmetic  25.9 us (3%)
  between operations  16.1 us (2%)
  local copies, waits for them, and re-layouts  10.9 us (1%)
    reduce_scatter x1, waiting for transfers between devices, body(): scatter(contract_first(hid, din).astype(BF), scatter_dimension=0)  169 us
    reduce_scatter x1, waiting for transfers between devices, body(): scatter(contract_first(act, g).astype(BF), scatter_dimension=1).astype(F32)  168 us
    pallas_call x1, Pallas kernels, run_block(): pl.pallas_call(block_kernel, out_shape=[full, full, full, jax.ShapeDtypeS...  160 us
    psum x1, blocking collectives, body(): small = lax.psum(small, ('fsdp', 'sp'))  146 us
    reduce_scatter x1, waiting for transfers between devices, body(): scatter(contract_first(hid, dproj).astype(BF), scatter_dimension=0)  66.3 us
    psum x1, waiting for transfers between devices, body(): lax.psum(mixed, 'tp').astype(F32)  59.2 us
    dot_general x4, matrix products, contract_first(): lax.dot_general(left, right, (((0,), (0,)), ((), ())), preferred_element_...  29.2 us
  transfers between devices with their start and end apart: 5, of which 4 were waited for; matrix products, arithmetic and copies ran while one was open for 6% of the time, Pallas kernels for 0%

profile of v1, /device:TPU:24, one launch (start us, length us, event | category | flops | bytes accessed | tf_op | source)
XLA Modules:
  0.0 850.4 jit_solution(6354907842335163864)
XLA Ops:
  8.0 0.0 all-reduce.3.cloned.1.call-start
  8.1 0.9 copy.32
  9.0 1.3 convert_element_type.64
  10.3 1.3 broadcast_in_dim.41
  11.6 0.7 convert_bitcast_fusion
  12.3 0.6 copy.33
  12.9 1.3 broadcast_in_dim.42
  14.2 1.6 pad_maximum_fusion.sa
  15.7 0.5 multiply_sine_fusion
  16.3 0.9 concatenate.19.cos
  17.2 0.8 pad_maximum_fusion.1.low
  18.1 0.9 concatenate.22.high
  18.9 159.5 %shard_map.211 = (bf16[512,2048]{1,0:T(8,128)(2,1)}, bf16[512,2048]{1,0:T(8,128)(2,1)}, bf16[512,2048]{1,0:T(8,128)(2,1)}, bf16[512,1536]{1,0:T(8,128)(2,1)}, bf...) custom-call(bf16[512,2048]{1,0:T(8,128)(2,1)} %bitcast.41, ...), custom_call_target="tpu_custom_call" | custom-call | flops 30000001024 | bytes 20000000 | tf_op jit(solution)/shard_map/pallas_call | solution.py:475
  178.5 0.0 all-reduce.3.cloned.1.call-update
  178.5 0.0 reduce-scatter.7.cloned.1.call-start
  178.6 1.5 copy-done.2
  180.1 0.1 copy-done.7
  180.1 2.6 convolution_convert_fusion.3
  182.8 0.0 reduce-scatter.7.cloned.1.call-update
  182.8 0.0 reduce-scatter.5.cloned.1.call-start
  182.8 8.2 convolution_convert_fusion.2
  191.0 0.0 reduce-scatter.5.cloned.1.call-update
  191.0 0.2 reduce-scatter.9.cloned.1.call-start
  191.3 10.0 %convolution_convert_fusion.1 = bf16[2048,2048]{1,0:T(8,128)(2,1)} fusion(bf16[512,2048]{1,0:T(8,128)(2,1)} %get-tuple-element.23, bf16[512,2048]{1,0:T(8,128)(2,1)} %get-tuple-element.26), kind=kOutput, calls=%fused_computation.1 | convolution fusion | flops 4299161600 | bytes 12582912 | tf_op jit(solution)/shard_map/dot_general | solution.py:498
  201.3 0.0 reduce-scatter.9.cloned.1.call-update
  201.3 0.0 reduce-scatter.11.cloned.1.call-start
  201.4 8.4 convolution_convert_fusion
  209.8 1.6 copy-done
  211.4 0.3 convert_reduce_fusion.1
  211.8 0.7 fusion.9
  212.5 0.8 slice_reduce_fusion
  213.3 0.9 fusion.14
  214.3 59.2 %all-reduce.3.cloned.1.call-done = (bf16[512,2048]{1,0:T(8,128)(2,1)}, bf16[512,2048]{1,0:T(8,128)(2,1)}) async-done(((bf16[512,2048]{1,0:T(8,128)(2,1)}, bf16[512,2048]{1,0:T(8,128)(2,1)}), (bf16[512,2048]{1,0:T(8,128)(2,1)}, bf16[512,2048]{1,0:T(8,128)(2,1)})) %all-reduce.3.cloned.1.call-update) | async-done | bytes 4194320 | tf_op jit(solution)/shard_map/psum | solution.py:522
  273.4 2.9 convert_reduce_fusion
  276.4 2.4 fusion.10
  278.8 146.1 %psum.23 = f32[9728]{0:T(1024)S(1)} all-reduce(f32[9728]{0:T(1024)S(1)} %constant_dynamic-update-slice_fusion), channel_id=1, replica_groups=mesh['fsdp'=4,'sp'=8,'tp'=4] {'fsdp','sp'}, use_global_device_ids=true, to_apply=%region_8.0 | all-reduce | flops 9728 | bytes 77824 | tf_op jit(solution)/shard_map/psum | solution.py:528
  424.9 0.6 slice.40
  425.5 0.6 fusion.15
  426.1 1.5 convert_element_type.76
  427.6 6.0 add_convert_fusion
  433.7 66.3 %reduce-scatter.5.cloned.1.call-done = bf16[64,1536]{1,0:T(8,128)(2,1)} async-done(((bf16[2048,1536]{1,0:T(8,128)(2,1)}), bf16[64,1536]{1,0:T(8,128)(2,1)}) %reduce-scatter.5.cloned.1.call-update) | async-done | bytes 196624 | tf_op jit(solution)/shard_map/reduce_scatter | solution.py:530
  499.9 1.0 reshape.134
  500.9 0.8 copy.37
  501.7 168.7 %reduce-scatter.9.cloned.1.call-done = bf16[64,2048]{1,0:T(8,128)(2,1)} async-done(((bf16[2048,2048]{1,0:T(8,128)(2,1)}), bf16[64,2048]{1,0:T(8,128)(2,1)}) %reduce-scatter.9.cloned.1.call-update) | async-done | bytes 262160 | tf_op jit(solution)/shard_map/reduce_scatter | solution.py:532
  670.4 1.8 convert_element_type.78
  672.2 168.1 %reduce-scatter.11.cloned.1.call-done = bf16[2048,64]{0,1:T(8,128)(2,1)} async-done(((bf16[2048,2048]{0,1:T(8,128)(2,1)}), bf16[2048,64]{0,1:T(8,128)(2,1)}) %reduce-scatter.11.cloned.1.call-update) | async-done | bytes 262160 | tf_op jit(solution)/shard_map/reduce_scatter | solution.py:533
  840.2 1.8 convert_element_type.80
  842.0 0.6 copy.45
  (35 shorter events, 0.2 us)
Async XLA Ops:
  8.0 265.4 %all-reduce.3.cloned.1.call-start = ((), (), s32[]{:S(2)}) async-start(), calls=%async_computation.8 | async-start | bytes 8388608 | tf_op jit(solution)/shard_map/psum | solution.py:522
  178.5 1.6 copy-start.2
  178.5 1.7 copy-start.7
  178.5 247.6 %reduce-scatter.7.cloned.1.call-start = ((), (), s32[]{:S(2)}) async-start(), calls=%async_computation.5 | async-start | bytes 2162688 | tf_op jit(solution)/shard_map/reduce_scatter | solution.py:531
  182.8 317.2 %reduce-scatter.5.cloned.1.call-start = ((), (), s32[]{:S(2)}) async-start(), calls=%async_computation.4 | async-start | bytes 6488064 | tf_op jit(solution)/shard_map/reduce_scatter | solution.py:530
  191.0 479.4 %reduce-scatter.9.cloned.1.call-start = ((), (), s32[]{:S(2)}) async-start(), calls=%async_computation.6 | async-start | bytes 8650752 | tf_op jit(solution)/shard_map/reduce_scatter | solution.py:532
  201.3 638.9 %reduce-scatter.11.cloned.1.call-start = ((), (), s32[]{:S(2)}) async-start(), calls=%async_computation.7 | async-start | bytes 8650752 | tf_op jit(solution)/shard_map/reduce_scatter | solution.py:533
  209.8 1.6 copy-start
  211.4 1.1 copy-start.5
  211.4 1.1 copy-start.6
  211.4 62.1 %copy-start.3 = (f32[2048]{0:T(1024)S(1)}, f32[2048]{0:T(1024)}, u32[]{:S(2)}) copy-start(f32[2048]{0:T(1024)} %convert_element_type.64) | copy-start | bytes 24580
  273.4 3.0 copy-start.1
  426.1 415.9 %copy-start.4 = (f32[2048]{0:T(1024)}, f32[2048]{0:T(1024)S(1)}, u32[]{:S(2)}) copy-start(f32[2048]{0:T(1024)S(1)} %get-tuple-element.108) | copy-start | bytes 24580
Sparse Core Ops, SparseCore 0:
  178.6 94.7 all-reduce.2
Sparse Core Ops, SparseCore 1:
  182.9 153.4 reduce-scatter.6
  338.6 161.3 reduce-scatter.4
  502.2 168.1 reduce-scatter.8
  672.8 167.3 reduce-scatter.10
